TPU v7x, 512 devices: a whole 4x8x8 slice. The times are simulated.
512 devices in a mesh: fsdp: 32 (over y, z_hi), tp: 16 (over x, z_lo, core).
Axes of the slice: x: 4, y: 8, z: 8 (z_hi: 4, z_lo: 2; z = z_hi * 2 + z_lo), core: 2. Of those that a mesh axis runs over, the one named last changes fastest.
Arguments:
- acts: bfloat16 [8192, 4096], P('fsdp'), may hold values from -6 to 6
- cots: bfloat16 [8192, 14336], P('fsdp', 'tp'), may hold values from -6 to 6
- weight: bfloat16 [4096, 14336], P('fsdp', 'tp'), may hold values from -0.09375 to 0.09375
- basis_in: bfloat16 [32, 128, 128], P('fsdp'), may hold values from -0.5 to 0.5
- basis_out: bfloat16 [16, 896, 896], P('tp', 'fsdp'), may hold values from -0.1875 to 0.1875
- eigen_in: float32 [4096], P('fsdp'), may hold values from 0.2 to 5
- eigen_out: float32 [14336], P('tp'), may hold values from 0.2 to 5
- forget_rows: int32 [2048], P('fsdp'), may hold values from 0 to 255
- retain_rows: int32 [1024], P('fsdp'), may hold values from 0 to 255
Outputs:
- retained: bfloat16 [1024, 14336], P('fsdp', 'tp')
- back_grads: bfloat16 [1024, 4096], P('fsdp')
All inputs are finite; a program needn't handle non-finite values.
Results may differ from a plain program's by a relative error of at most 0.022.
Values may be sent and summed in bfloat16 or wider, within the bound.
A program may use at most 64 MiB of HBM per device.

v0:
```python
import jax
import jax.numpy as jnp
from jax import lax
from jax.sharding import PartitionSpec as P

damping = 0.1
step_size = 0.5


def shards(acts, cots, weight, basis_in, basis_out, eigen_in, eigen_out, forget_rows, retain_rows):
    fsdp_count = lax.axis_size("fsdp")
    forget_local = forget_rows.shape[0]
    forget_count = forget_local * fsdp_count
    row_count = weight.shape[0]
    col_count = weight.shape[1]
    in_blocks = basis_in.shape[0]
    in_order = basis_in.shape[1]
    forget_acts = jnp.take(acts, forget_rows, axis=0)
    forget_cots = jnp.take(cots, forget_rows, axis=0)
    basis_full = lax.all_gather(basis_out, "fsdp", axis=1, tiled=True)
    out_blocks = basis_full.shape[0]
    out_order = basis_full.shape[2]
    rotated_cots = (
        jnp.einsum(
            "tgi,gij->tgj",
            forget_cots.reshape(forget_local, out_blocks, out_order),
            basis_full,
            preferred_element_type=jnp.float32,
        )
        .reshape(forget_local, col_count)
        .astype(jnp.bfloat16)
    )
    feature_cols = lax.all_to_all(forget_acts, "fsdp", split_axis=1, concat_axis=0, tiled=True)
    rotated_acts = (
        jnp.einsum(
            "tbi,bij->tbj",
            feature_cols.reshape(forget_count, in_blocks, in_order),
            basis_in,
            preferred_element_type=jnp.float32,
        )
        .reshape(forget_count, row_count)
        .astype(jnp.bfloat16)
    )
    moments = (
        lax.dot_general(
            rotated_acts,
            lax.all_gather(rotated_cots, "fsdp", axis=0, tiled=True),
            (((0,), (0,)), ((), ())),
            preferred_element_type=jnp.float32,
        )
        / forget_count
    )
    damped = eigen_in[:, None] * eigen_out[None, :] + damping
    scaled = (moments / damped).astype(jnp.bfloat16)
    back_out = (
        jnp.einsum(
            "dgi,gji->dgj",
            scaled.reshape(row_count, out_blocks, out_order),
            basis_full,
            preferred_element_type=jnp.float32,
        )
        .reshape(row_count, col_count)
        .astype(jnp.bfloat16)
    )
    update = jnp.einsum(
        "bij,bjc->bic",
        basis_in,
        back_out.reshape(in_blocks, in_order, col_count),
        preferred_element_type=jnp.float32,
    ).reshape(row_count, col_count)
    new_weight = (weight.astype(jnp.float32) + step_size * update).astype(jnp.bfloat16)
    retain_acts = jnp.take(acts, retain_rows, axis=0)
    retain_cots = jnp.take(cots, retain_rows, axis=0)
    retain_cols = lax.all_to_all(retain_acts, "fsdp", split_axis=1, concat_axis=0, tiled=True)
    retained = lax.psum_scatter(
        jnp.dot(retain_cols, new_weight, preferred_element_type=jnp.float32).astype(jnp.bfloat16),
        "fsdp",
        scatter_dimension=0,
        tiled=True,
    )
    grad_cols = lax.dot_general(
        lax.all_gather(retain_cots, "fsdp", axis=0, tiled=True),
        new_weight,
        (((1,), (1,)), ((), ())),
        preferred_element_type=jnp.float32,
    )
    grad_summed = lax.psum(grad_cols.astype(jnp.bfloat16), "tp")
    back_grads = lax.all_to_all(grad_summed, "fsdp", split_axis=0, concat_axis=1, tiled=True)
    return (retained, back_grads)


def solution(mesh):
    placed = (
        P("fsdp", None),
        P("fsdp", "tp"),
        P("fsdp", "tp"),
        P("fsdp", None, None),
        P("tp", "fsdp", None),
        P("fsdp"),
        P("tp"),
        P("fsdp"),
        P("fsdp"),
    )
    return jax.shard_map(
        shards,
        mesh=mesh,
        in_specs=placed,
        out_specs=(P("fsdp", "tp"), P("fsdp", None)),
        check_vma=False,
    )
```

profile of v0, /device:TPU:1, one launch (start us, length us, event | category | flops | bytes accessed | tf_op | source)
XLA Modules:
  0.0 663.0 jit_solution(1411980744719282719)
XLA Ops:
  7.2 0.0 copy-start
  7.2 0.0 copy-start.1
  7.2 0.0 copy-start.5
  7.2 0.0 all-gather.4.cloned.1.call-start
  7.2 1.7 copy.25
  8.9 0.0 all-gather.4.cloned.1.call-update
  9.0 0.0 all-gather.6.cloned.1.call-start
  9.0 0.7 compare_select_fusion
  9.7 1.9 gather_fusion.2
  11.5 0.7 compare_and_fusion
  12.2 98.4 %all-gather.4.cloned.1.call-done = bf16[1,896,896]{2,0,1:T(2,128)(2,1)} async-done(((bf16[1,28,896]{2,0,1:T(2,128)(2,1)}), bf16[1,896,896]{2,0,1:T(2,128)(2,1)}) %all-gather.4.cloned.1.call-update) | async-done | bytes 1605648 | tf_op jit(solution)/shard_map/all_gather | solution.py:20
  110.6 3.0 fusion.16
  113.6 0.0 all-gather.6.cloned.1.call-update
  113.6 0.0 all-gather.8.cloned.1.call-start
  113.6 0.0 copy-done.5
  113.7 0.0 copy-done.1
  113.7 0.6 gather_fusion.3
  114.3 0.7 broadcast_select_fusion
  115.0 0.0 all-gather.8.cloned.1.call-update
  115.1 0.0 copy-done
  115.1 0.9 gather_fusion.1
  115.9 0.0 copy-start.2
  116.0 1.1 bitcast_select_fusion
  117.0 6.5 all-to-all-start.1
  123.5 0.0 copy-start.3
  123.5 0.0 copy-start.4
  123.5 0.0 copy-start.6
  123.5 0.7 gather_fusion
  124.2 0.0 copy-done.2
  124.3 0.2 copy.23
  124.4 0.8 bitcast_select_fusion.1
  125.3 14.6 %all-to-all-done.1 = bf16[64,32,128]{2,0,1:T(8,128)(2,1)S(1)} async-done(((bf16[64,32,128]{2,0,1:T(8,128)(2,1)}), bf16[64,32,128]{2,0,1:T(8,128)(2,1)S(1)}, u32[]{:S(2)}, u32[]{:S(2)}) %all-to-all-start.1) | async-done | bytes 524320 | tf_op jit(solution)/shard_map/all_to_all | solution.py:33
  139.8 8.0 %all-to-all-start = ((bf16[32,32,128]{2,0,1:T(8,128)(2,1)}), bf16[32,32,128]{2,0,1:T(8,128)(2,1)S(1)}, u32[]{:S(2)}, u32[]{:S(2)}) async-start(bf16[32,32,128]{2,0,1:T(8,128)(2,1)} %bitcast_select_fusion.1), calls=%async_computation | async-start | bytes 524288 | tf_op jit(solution)/shard_map/all_to_all | solution.py:74
  147.9 0.0 all-reduce.2.cloned.1.call-start
  147.9 67.0 %all-gather.6.cloned.1.call-done = bf16[2048,896]{1,0:T(8,128)(2,1)} async-done(((bf16[64,896]{1,0:T(8,128)(2,1)}), bf16[2048,896]{1,0:T(8,128)(2,1)}) %all-gather.6.cloned.1.call-update) | async-done | bytes 3670032 | tf_op jit(solution)/shard_map/all_gather | solution.py:47
  214.9 0.0 copy-done.3
  214.9 0.0 copy-done.4
  214.9 0.0 copy-done.6
  214.9 3.0 fusion.13
  218.0 2.8 fusion.12
  220.8 77.6 %all-gather.8.cloned.1.call-done = bf16[1024,896]{1,0:T(8,128)(2,1)} async-done(((bf16[32,896]{1,0:T(8,128)(2,1)}), bf16[1024,896]{1,0:T(8,128)(2,1)}) %all-gather.8.cloned.1.call-update) | async-done | bytes 1835024 | tf_op jit(solution)/shard_map/all_gather | solution.py:82
  298.4 2.9 convolution_convert_fusion.2
  301.3 0.0 all-reduce.2.cloned.1.call-update
  301.3 0.0 reduce-scatter.2.cloned.1.call-start
  301.3 0.0 all-to-all-done
  301.3 1.9 convolution_convert_fusion.1
  303.2 0.0 reduce-scatter.2.cloned.1.call-update
  303.3 124.3 %all-reduce.2.cloned.1.call-done = bf16[32,32,128]{2,1,0:T(8,128)(2,1)} async-done(((bf16[32,32,128]{2,1,0:T(8,128)(2,1)}), bf16[32,32,128]{2,1,0:T(8,128)(2,1)}) %all-reduce.2.cloned.1.call-update) | async-done | bytes 262160 | tf_op jit(solution)/shard_map/psum | solution.py:87
  427.6 23.0 %all_to_all.48 = bf16[32,32,128]{2,1,0:T(8,128)(2,1)S(1)} all-to-all(bf16[32,32,128]{2,1,0:T(8,128)(2,1)} %all-reduce.2.cloned.1.call-done), channel_id=1, replica_groups=mesh['fsdp'=32,'tp'=16] {'fsdp'}, dimensions={0} | all-to-all | bytes 524288 | tf_op jit(solution)/shard_map/all_to_all | solution.py:88
  450.6 0.7 copy_bitcast_fusion
  451.4 205.1 %reduce-scatter.2.cloned.1.call-done = bf16[32,896]{1,0:T(8,128)(2,1)} async-done(((bf16[1024,896]{1,0:T(8,128)(2,1)}), bf16[32,896]{1,0:T(8,128)(2,1)}) %reduce-scatter.2.cloned.1.call-update) | async-done | bytes 57360 | tf_op jit(solution)/shard_map/reduce_scatter | solution.py:75
  (4 shorter events, 0.0 us)
Async XLA Ops:
  7.2 107.9 %copy-start = (bf16[256,4096]{1,0:T(8,128)(2,1)S(1)}, bf16[256,4096]{1,0:T(8,128)(2,1)}, u32[]{:S(2)}) copy-start(bf16[256,4096]{1,0:T(8,128)(2,1)} %param.9) | copy-start | bytes 6291460
  7.2 106.5 %copy-start.1 = (bf16[256,896]{1,0:T(8,128)(2,1)S(1)}, bf16[256,896]{1,0:T(8,128)(2,1)}, u32[]{:S(2)}) copy-start(bf16[256,896]{1,0:T(8,128)(2,1)} %param.10) | copy-start | bytes 1376260
  7.2 106.5 %copy-start.5 = (s32[32]{0:T(128)S(1)}, s32[32]{0:T(128)}, u32[]{:S(2)}) copy-start(s32[32]{0:T(128)} %param.17) | copy-start | bytes 388
  7.2 103.4 %all-gather.4.cloned.1.call-start = ((), (), s32[]{:S(2)}) async-start(), calls=%async_computation.4 | async-start | bytes 3311616 | tf_op jit(solution)/shard_map/all_gather | solution.py:20
  9.0 206.0 %all-gather.6.cloned.1.call-start = ((), (), s32[]{:S(2)}) async-start(), calls=%async_computation.5 | async-start | bytes 3784704 | tf_op jit(solution)/shard_map/all_gather | solution.py:47
  113.6 184.8 %all-gather.8.cloned.1.call-start = ((), (), s32[]{:S(2)}) async-start(), calls=%async_computation.7 | async-start | bytes 1892352 | tf_op jit(solution)/shard_map/all_gather | solution.py:82
  115.9 8.3 %copy-start.2 = (bf16[128,896]{1,0:T(8,128)(2,1)S(1)}, bf16[128,896]{1,0:T(8,128)(2,1)}, u32[]{:S(2)}) copy-start(bf16[128,896]{1,0:T(8,128)(2,1)} %param.11) | copy-start | bytes 688132
  117.0 22.8 %all-to-all-start.1 = ((bf16[64,32,128]{2,0,1:T(8,128)(2,1)}), bf16[64,32,128]{2,0,1:T(8,128)(2,1)S(1)}, u32[]{:S(2)}, u32[]{:S(2)}) async-start(bf16[64,32,128]{2,0,1:T(8,128)(2,1)} %bitcast_select_fusion), calls=%async_computation.1 | async-start | bytes 1048576 | tf_op jit(solution)/shard_map/all_to_all | solution.py:33
  123.5 91.4 %copy-start.3 = (bf16[1,128,128]{2,1,0:T(8,128)(2,1)S(1)}, bf16[1,128,128]{2,1,0:T(8,128)(2,1)}, u32[]{:S(2)}) copy-start(bf16[1,128,128]{2,1,0:T(8,128)(2,1)} %param.12) | copy-start | bytes 98308
  123.5 91.4 %copy-start.4 = (f32[896]{0:T(1024)S(1)}, f32[896]{0:T(1024)}, u32[]{:S(2)}) copy-start(f32[896]{0:T(1024)} %param.15) | copy-start | bytes 10756
  123.5 91.4 %copy-start.6 = (f32[128]{0:T(128)S(1)}, f32[128]{0:T(128)}, u32[]{:S(2)}) copy-start(f32[128]{0:T(128)} %param.14) | copy-start | bytes 1540
  139.8 161.5 %all-to-all-start = ((bf16[32,32,128]{2,0,1:T(8,128)(2,1)}), bf16[32,32,128]{2,0,1:T(8,128)(2,1)S(1)}, u32[]{:S(2)}, u32[]{:S(2)}) async-start(bf16[32,32,128]{2,0,1:T(8,128)(2,1)} %bitcast_select_fusion.1), calls=%async_computation | async-start | bytes 524288 | tf_op jit(solution)/shard_map/all_to_all | solution.py:74
  147.9 279.7 %all-reduce.2.cloned.1.call-start = ((), (), s32[]{:S(2)}) async-start(), calls=%async_computation.8 | async-start | bytes 524288 | tf_op jit(solution)/shard_map/psum | solution.py:87
  301.3 355.2 %reduce-scatter.2.cloned.1.call-start = ((), (), s32[]{:S(2)}) async-start(), calls=%async_computation.6 | async-start | bytes 1892352 | tf_op jit(solution)/shard_map/reduce_scatter | solution.py:75
Sparse Core Ops, SparseCore 0:
  11.7 98.8 all-gather.3
  113.8 101.1 all-gather.5
  218.7 79.6 all-gather.7
  301.4 126.1 all-reduce.1
  433.1 223.2 reduce-scatter.1
where the time goes:
time: 667 us; the launch traced here: 663 us
  waiting for transfers between devices  587 us (88%)
  blocking collectives  23 us (3%)
  starting transfers between devices  14.7 us (2%)
  between operations  13.9 us (2%)
  matrix products  13.5 us (2%)
  local copies, waits for them, and re-layouts  6.7 us (1%)
    reduce_scatter x1, waiting for transfers between devices, shards(): lax.psum_scatter(jnp.dot(retain_cols, new_weight, preferred_element_type=...  205 us
    psum x1, waiting for transfers between devices, shards(): grad_summed = lax.psum(grad_cols.astype(jnp.bfloat16), 'tp')  124 us
    all_gather x1, waiting for transfers between devices, shards(): basis_full = lax.all_gather(basis_out, 'fsdp', axis=1, tiled=True)  98.4 us
    all_gather x1, waiting for transfers between devices, shards(): lax.all_gather(retain_cots, 'fsdp', axis=0, tiled=True)  77.6 us
    all_gather x1, waiting for transfers between devices, shards(): lax.all_gather(rotated_cots, 'fsdp', axis=0, tiled=True)  67 us
    all_to_all x1, blocking collectives, shards(): lax.all_to_all(grad_summed, 'fsdp', split_axis=0, concat_axis=1, tiled=True)  23 us
    all_to_all x1, waiting for transfers between devices, shards(): lax.all_to_all(forget_acts, 'fsdp', split_axis=1, concat_axis=0, tiled=True)  14.6 us
  transfers between devices with their start and end apart: 7, of which 6 were waited for; matrix products, arithmetic and copies ran while one was open for 3% of the time, Pallas kernels for 0%

commit v1 on v0

v1 whole, which is shorter than its diff:
```python
import functools

import jax
import jax.numpy as jnp
from jax import lax
from jax.experimental import pallas as pl
from jax.experimental.pallas import tpu as pltpu
from jax.sharding import PartitionSpec as P

damping = 0.1
step_size = 0.5
MESH = pl.DeviceIdType.MESH
BF = jnp.bfloat16
F32 = jnp.float32
NY, NH, NX, NC = 8, 4, 4, 4


def dot(a, b, ca, cb):
    return lax.dot_general(a, b, (((ca,), (cb,)), ((), ())), preferred_element_type=F32)


def body(fc, rc, cols, dblk, brows, forget_count,
         acts, cots, weight, basis_in, basis_out, eigen_in, eigen_out, frow, rrow,
         out_r, out_g,
         af, ar, asf, asr, cf, cr, bz, b112, bb, ts, tr, nw, rs, rr, gs, gr, g2, g3, go,
         ssem, rsem):
    f = lax.axis_index("fsdp")
    t = lax.axis_index("tp")
    y, h = f // NH, f % NH
    x, c = t // NC, t % NC

    def ydev(k):
        return (((y + k) % NY) * NH + h, t)

    def hdev(k):
        return (y * NH + (h + k) % NH, t)

    def tdev(k):
        return (f, (t + k) % 16)

    ypeers = [ydev(k) for k in range(1, NY)]
    hpeers = [hdev(k) for k in range(1, NH)]
    tpeers = [tdev(k) for k in range(1, 16)]
    bar = pltpu.get_barrier_semaphore()
    for p in ypeers + hpeers + tpeers:
        pl.semaphore_signal(bar, inc=1, device_id=p, device_id_type=MESH)

    count = [0]

    def sems(n):
        i = count[0]
        count[0] += n
        return i

    def rcopy(src, dst, i, dev):
        return pltpu.make_async_remote_copy(
            src_ref=src, dst_ref=dst, send_sem=ssem.at[i], recv_sem=rsem.at[i],
            device_id=dev, device_id_type=MESH)

    def rows_of(slot, n):
        return pl.ds(pl.multiple_of(slot * n, 16), n)

    pending = []

    class Ring:
        def __init__(self, buf, rows, cut):
            self.buf, self.rows, self.cut = buf, rows, cut
            self.base = sems(8)
            self.cps = [[], []]

        def send(self, s):
            for d in range(2):
                if s:
                    self.cps[d][s - 1].wait_recv()
                slot = (y - s) % NY if d == 0 else (y + s) % NY
                if s == 3:
                    lo, n = (0, self.cut) if d == 0 else (self.cut, self.rows - self.cut)
                else:
                    lo, n = 0, self.rows
                sl = pl.ds(pl.multiple_of(slot * self.rows + lo, 16), n)
                cp = rcopy(self.buf.at[sl], self.buf.at[sl], self.base + d * 4 + s, ydev(1 if d == 0 else NY - 1))
                cp.start()
                self.cps[d].append(cp)
                pending.append(cp)

        def finish(self):
            for d in range(2):
                self.cps[d][3].wait_recv()

    pool = acts.shape[0]
    ohf = (lax.broadcasted_iota(jnp.int32, (pool, fc), 0) == frow[...]).astype(BF)
    ohr = (lax.broadcasted_iota(jnp.int32, (pool, rc), 0) == rrow[...]).astype(BF)
    cf[rows_of(y, fc), :] = dot(ohf, cots[...], 0, 0).astype(BF)
    bz[pl.ds(pl.multiple_of(h * 32, 16), 32), :] = jnp.zeros((32, cols), BF)
    bz[pl.ds(pl.multiple_of(h * 32, 16), brows), :] = basis_out[0]

    pl.semaphore_wait(bar, len(ypeers) + len(hpeers) + len(tpeers))

    ring_cf = Ring(cf, fc, fc // 2)
    ring_cf.send(0)

    ib = sems(3)
    bcps = []
    for k in range(1, NH):
        sl = pl.ds(pl.multiple_of(h * 32, 16), 32)
        cp = rcopy(bz.at[sl], bz.at[sl], ib + k - 1, hdev(k))
        cp.start()
        bcps.append(cp)
        pending.append(cp)

    for j in range(NY):
        asf[j] = dot(ohf, acts[:, j * dblk:(j + 1) * dblk], 0, 0).astype(BF)
    ia = sems(7)
    acps = []
    for k in (1, 7, 2, 6, 3, 5, 4):
        cp = rcopy(asf.at[(y + k) % NY], af.at[rows_of(y, fc)], ia + k - 1, ydev(k))
        cp.start()
        acps.append(cp)
        pending.append(cp)
    af[rows_of(y, fc), :] = asf[y]

    ring_cf.send(1)
    cr[rows_of(y, rc), :] = dot(ohr, cots[...], 0, 0).astype(BF)
    for j in range(NY):
        asr[j] = dot(ohr, acts[:, j * dblk:(j + 1) * dblk], 0, 0).astype(BF)
    ring_cf.send(2)
    ring_cf.send(3)

    for cp in bcps:
        cp.wait_recv()
    parts = [bz[k * 32:k * 32 + brows, :].astype(F32) for k in range(NH)]
    b112[...] = jnp.concatenate(parts, axis=0)
    bb[rows_of(y, NH * brows), :] = b112[...].astype(BF)
    ring_b = Ring(bb, NH * brows, 64)
    ring_b.send(0)

    for cp in acps:
        cp.wait_recv()
    ring_cf.finish()

    for q in range(NH):
        ts[q] = dot(af[:, q * 128:(q + 1) * 128], cf[...], 0, 0).astype(BF)
    it = sems(3)
    tcps = []
    for k in (1, 3, 2):
        cp = rcopy(ts.at[(h + k) % NH], tr.at[k - 1], it + k - 1, hdev(k))
        cp.start()
        tcps.append(cp)
        pending.append(cp)

    ring_b.send(1)
    ring_cr = Ring(cr, rc, rc // 2)
    ring_cr.send(0)
    ia = sems(7)
    rcps = []
    for k in (1, 7, 2, 6, 3, 5, 4):
        cp = rcopy(asr.at[(y + k) % NY], ar.at[rows_of(y, rc)], ia + k - 1, ydev(k))
        cp.start()
        rcps.append(cp)
        pending.append(cp)
    ar[rows_of(y, rc), :] = asr[y]
    ring_b.send(2)
    ring_cr.send(1)
    ring_b.send(3)
    ring_cr.send(2)
    ring_cr.send(3)

    for cp in tcps:
        cp.wait_recv()
    mom = ts[h].astype(F32) + tr[0].astype(F32) + tr[1].astype(F32) + tr[2].astype(F32)
    q_in = basis_in[0]
    rot = dot(q_in, mom.astype(BF), 0, 0).astype(BF)
    ring_b.finish()
    m2 = dot(rot, bb[...], 1, 0) / forget_count
    eye = lax.broadcasted_iota(jnp.int32, (128, 128), 0) == lax.broadcasted_iota(jnp.int32, (128, 128), 1)
    ein = jnp.sum(jnp.where(eye, eigen_in[...], 0.0), axis=1, keepdims=True)
    scaled = (m2 / (ein * eigen_out[...] + damping)).astype(BF)
    back = dot(scaled, bb[...], 1, 1).astype(BF)
    upd = dot(q_in, back, 1, 0)
    nw[rows_of(h, 128), :] = (weight[...].astype(F32) + step_size * upd).astype(BF)

    iw = sems(3)
    wcps = []
    for k in (1, 3, 2):
        cp = rcopy(nw.at[rows_of(h, 128)], nw.at[rows_of(h, 128)], iw + k - 1, hdev(k))
        cp.start()
        wcps.append(cp)
        pending.append(cp)
    for cp in rcps:
        cp.wait_recv()
    ring_cr.finish()
    for cp in wcps:
        cp.wait_recv()

    for q in range(NH):
        g = dot(cr[...], nw[q * 128:(q + 1) * 128, :], 1, 1)
        for r in range(NC):
            gs[q * NC + r] = g[r * 64:(r + 1) * 64, :].astype(BF)
    ig = sems(15)
    gcps = []
    for k in range(1, 16):
        cp = rcopy(gs.at[(t + k) % 16], gr.at[k - 1], ig + k - 1, tdev(k))
        cp.start()
        gcps.append(cp)
        pending.append(cp)

    for j in range(NY):
        rs[j] = dot(ar[j * rc:(j + 1) * rc, :], nw[...], 1, 0).astype(BF)
    ir = sems(7)
    scps = []
    for k in (1, 7, 2, 6, 3, 5, 4):
        cp = rcopy(rs.at[(y + k) % NY], rr.at[k - 1], ir + k - 1, ydev(k))
        cp.start()
        scps.append(cp)
        pending.append(cp)

    for cp in gcps:
        cp.wait_recv()
    tot = gs[t].astype(F32)
    for k in range(15):
        tot = tot + gr[k].astype(F32)
    g2[...] = tot.astype(BF)

    i2 = sems(8)
    s2 = sems(2)
    for i in range(2):
        yo = 2 * c + i
        k = (yo - y) % NY

        def copy2():
            return pltpu.make_async_remote_copy(
                src_ref=g2.at[pl.ds(i * rc, rc)], dst_ref=g3.at[y],
                send_sem=ssem.at[s2 + i], recv_sem=rsem.at[i2 + k],
                device_id=(yo * NH + h, t), device_id_type=MESH)

        @pl.when(k != 0)
        def _():
            copy2().start()

        @pl.when(k == 0)
        def _():
            g3[y] = g2[i * rc:(i + 1) * rc, :]

    i3 = sems(4)
    s3 = sems(15)
    mine = (y // 2) == c

    @pl.when(mine)
    def _():
        for k in range(1, NY):
            rcopy(g2.at[pl.ds(0, rc)], g3.at[y], i2 + k, ydev(k)).wait_recv()
        for k in range(1, 16):
            pltpu.make_async_remote_copy(
                src_ref=g3, dst_ref=go.at[x], send_sem=ssem.at[s3 + k - 1],
                recv_sem=rsem.at[i3 + x], device_id=tdev(k), device_id_type=MESH).start()
        go[x] = g3[...]

    for cp in scps:
        cp.wait_recv()
    tot = rs[y].astype(F32)
    for k in range(7):
        tot = tot + rr[k].astype(F32)
    out_r[...] = tot.astype(BF)

    for i in range(2):
        yo = 2 * c + i

        @pl.when(yo != y)
        def _():
            pltpu.make_async_remote_copy(
                src_ref=g2.at[pl.ds(i * rc, rc)], dst_ref=g3.at[y],
                send_sem=ssem.at[s2 + i], recv_sem=rsem.at[i2],
                device_id=(yo * NH + h, t), device_id_type=MESH).wait_send()

    for xs in range(NX):
        @pl.when(jnp.logical_not(jnp.logical_and(mine, x == xs)))
        def _():
            pltpu.make_async_remote_copy(
                src_ref=g3, dst_ref=go.at[xs], send_sem=ssem.at[s3],
                recv_sem=rsem.at[i3 + xs], device_id=tdev(1), device_id_type=MESH).wait_recv()
    for q in range(NX):
        for j in range(NY):
            lo = j * dblk + q * 128
            out_g[:, lo:lo + 128] = go[q, j]

    @pl.when(mine)
    def _():
        for k in range(1, 16):
            pltpu.make_async_remote_copy(
                src_ref=g3, dst_ref=go.at[x], send_sem=ssem.at[s3 + k - 1],
                recv_sem=rsem.at[i3], device_id=tdev(k), device_id_type=MESH).wait_send()
    for cp in pending:
        cp.wait_send()
    assert count[0] <= 120


def shards(acts, cots, weight, basis_in, basis_out, eigen_in, eigen_out, forget_rows, retain_rows):
    fc, rc = forget_rows.shape[0], retain_rows.shape[0]
    cols = cots.shape[1]
    dim = acts.shape[1]
    dblk = dim // NY
    brows = basis_out.shape[1]
    vm = lambda *s: pltpu.VMEM(s, BF)
    kern = functools.partial(body, fc, rc, cols, dblk, brows, float(fc * NY * NH))
    return pl.pallas_call(
        kern,
        out_shape=(jax.ShapeDtypeStruct((rc, cols), BF), jax.ShapeDtypeStruct((rc, dim), BF)),
        in_specs=[pl.BlockSpec(memory_space=pltpu.VMEM)] * 9,
        out_specs=(pl.BlockSpec(memory_space=pltpu.VMEM),) * 2,
        scratch_shapes=[
            vm(NY * fc, dblk), vm(NY * rc, dblk), vm(NY, fc, dblk), vm(NY, rc, dblk),
            vm(NY * fc, cols), vm(NY * rc, cols),
            vm(NH * 32, cols), pltpu.VMEM((NH * brows, cols), F32), vm(cols, cols),
            vm(NH, 128, cols), vm(NH - 1, 128, cols), vm(NH * 128, cols),
            vm(NY, rc, cols), vm(NY - 1, rc, cols),
            vm(16, 64, 128), vm(15, 64, 128), vm(64, 128), vm(NY, rc, 128), vm(NX, NY, rc, 128),
            pltpu.SemaphoreType.DMA((120,)), pltpu.SemaphoreType.DMA((120,)),
        ],
        compiler_params=pltpu.CompilerParams(collective_id=0, has_side_effects=True, vmem_limit_bytes=50 * 2**20),
        name="newton_step",
    )(acts, cots, weight, basis_in, basis_out, eigen_in.reshape(1, -1), eigen_out.reshape(1, -1),
      forget_rows.reshape(1, -1), retain_rows.reshape(1, -1))


def solution(mesh):
    placed = (
        P("fsdp", None),
        P("fsdp", "tp"),
        P("fsdp", "tp"),
        P("fsdp", None, None),
        P("tp", "fsdp", None),
        P("fsdp"),
        P("tp"),
        P("fsdp"),
        P("fsdp"),
    )
    return jax.shard_map(
        shards,
        mesh=mesh,
        in_specs=placed,
        out_specs=(P("fsdp", "tp"), P("fsdp", None)),
        check_vma=False,
    )
```

time: 667 us -> 118 us (0.18)
  waiting for transfers between devices: 587 us -> 0 us
  Pallas kernels: 0 us -> 106 us
  blocking collectives: 23 us -> 0 us
  starting transfers between devices: 14.7 us -> 0 us
  matrix products: 13.5 us -> 0 us
  between operations: 13.9 us -> 0.65 us
    all_gather x3 -> x0, waiting for transfers between devices: 243 us -> none  [the longest x1 98.4 us: shards(): basis_full = lax.all_gather(basis_out, 'fsdp', axis=1, tiled=True)]
    reduce_scatter x1 -> x0, waiting for transfers between devices: 205 us -> none  [shards(): lax.psum_scatter(jnp.dot(retain_cols, new_weight, preferred_element_type=...]
    psum x1 -> x0, waiting for transfers between devices: 124 us -> none  [shards(): grad_summed = lax.psum(grad_cols.astype(jnp.bfloat16), 'tp')]
    pallas_call x0 -> x1, Pallas kernels: none -> 106 us  [shards(): pl.pallas_call(kern, out_shape=(jax.ShapeDtypeStruct((rc, cols), BF), jax...]
    all_to_all x1 -> x0, blocking collectives: 23 us -> none  [shards(): lax.all_to_all(grad_summed, 'fsdp', split_axis=0, concat_axis=1, tiled=True)]
    all_to_all x2 -> x0, waiting for transfers between devices: 14.6 us -> none  [the longest x1 14.6 us: shards(): lax.all_to_all(forget_acts, 'fsdp', split_axis=1, concat_axis=0, tiled=True)]
    all_to_all x2 -> x0, starting transfers between devices: 14.5 us -> none  [the longest x1 8.03 us: shards(): lax.all_to_all(retain_acts, 'fsdp', split_axis=1, concat_axis=0, tiled=True)]
    dot_general x5 -> x0, matrix products: 13.5 us -> none  [the longest x1 3.04 us: shards(): lax.dot_general(rotated_acts, lax.all_gather(rotated_cots, 'fsdp', axis=0...]
  transfers between devices with their start and end apart: 7 -> 0, of which waited for: 6 -> 0; matrix products, arithmetic and copies ran while one was open for 3% -> 0% of each run, Pallas kernels for 0% -> 0%
where the time goes in v1:
time: 118 us; the launch traced here: 116 us
  Pallas kernels  106 us (90%)
  local copies, waits for them, and re-layouts  9.1 us (8%)
    pallas_call x1, Pallas kernels, shards(): pl.pallas_call(kern, out_shape=(jax.ShapeDtypeStruct((rc, cols), BF), jax...  106 us
    unnamed x18, local copies, waits for them, and re-layouts  8.41 us

profile of v1, /device:TPU:1, one launch (start us, length us, event | category | flops | bytes accessed | tf_op | source)
XLA Modules:
  0.0 116.2 jit_solution(3210630059827784769)
XLA Ops:
  0.6 0.7 reshape.17.eigen_out
  1.3 0.0 copy-start
  1.3 1.6 %copy-done = bf16[256,4096]{1,0:T(8,128)(2,1)S(1)} copy-done((bf16[256,4096]{1,0:T(8,128)(2,1)S(1)}, bf16[256,4096]{1,0:T(8,128)(2,1)}, u32[]{:S(2)}) %copy-start) | copy-done | bytes 2097176
  2.9 0.0 copy-start.1
  2.9 1.0 copy-done.1
  3.9 0.0 copy-start.2
  3.9 0.9 copy-done.2
  4.9 0.0 copy-start.3
  4.9 0.8 copy-done.3
  5.7 0.0 copy-start.4
  5.7 0.8 copy-done.4
  6.4 0.0 copy-start.5
  6.5 0.7 copy-done.5
  7.1 0.0 copy-start.6
  7.1 0.7 copy-done.6
  7.8 0.0 copy-start.7
  7.8 0.7 copy-done.7
  8.4 106.4 %newton_step.1 = (bf16[32,896]{1,0:T(8,128)(2,1)S(1)}, bf16[32,4096]{1,0:T(8,128)(2,1)S(1)}) custom-call(bf16[256,4096]{1,0:T(8,128)(2,1)S(1)} %copy-done, bf16[256,896]{1,0:T(8,128)(2,1)S(1)} %copy-done.1, bf16[128,896]{1,0:T(8,128)(2,1)S(1)} %copy-done.2, bf16[1,128,128]{2,1,0:T(8,128)(2,1)S(1)} %copy-done.4, bf16[1,28,896]{2,1,0:T(8,128)(2,1)S(1)} %copy-done.3, ...), custom_call_target="tpu_custom_call" | custom-call | tf_op jit(solution)/shard_map/newton_step/pallas_call | solution.py:305
  114.8 0.6 copy.13
  115.4 0.7 copy.14
Async XLA Ops:
  1.3 1.6 %copy-start = (bf16[256,4096]{1,0:T(8,128)(2,1)S(1)}, bf16[256,4096]{1,0:T(8,128)(2,1)}, u32[]{:S(2)}) copy-start(bf16[256,4096]{1,0:T(8,128)(2,1)} %acts.1) | copy-start | bytes 6291460
  2.9 1.0 copy-start.1
  3.9 0.9 copy-start.2
  4.9 0.8 copy-start.3
  5.7 0.8 copy-start.4
  6.4 0.7 copy-start.5
  7.1 0.7 copy-start.6
  7.8 0.7 copy-start.7

commit v2 on v0

v2 whole, which is shorter than its diff:
```python
import functools

import jax
import jax.numpy as jnp
from jax import lax
from jax.experimental import pallas as pl
from jax.experimental.pallas import tpu as pltpu
from jax.sharding import PartitionSpec as P

damping = 0.1
step_size = 0.5
MESH = pl.DeviceIdType.MESH
BF = jnp.bfloat16
F32 = jnp.float32
NY, NH, NX, NC = 8, 4, 4, 4
NSEM = 200


def dot(a, b, ca, cb):
    return lax.dot_general(a, b, (((ca,), (cb,)), ((), ())), preferred_element_type=F32)


def body(fc, rc, cols, dblk, brows, forget_count,
         acts_in, cots_in, weight_in, basis_in_in, basis_out_in, eigen_in_in, eigen_out_in, frow_in, rrow_in,
         out_r, out_g,
         acb, cots, weight, basis_in, bsrc, ein_v, eout_v, frow, rrow,
         af, ar, asf, asr, cf, cr, bz, b112, bb, ts, tf, tg, tr, nw, rs, rr, gs, gr, g2, g3, go,
         lsem, ssem, rsem):
    f = lax.axis_index("fsdp")
    t = lax.axis_index("tp")
    y, h = f // NH, f % NH
    x, c = t // NC, t % NC
    half, core = c // 2, c % 2

    def dev(h_, x_, c_):
        return (y * NH + h_, x_ * NC + c_)

    def ydev(k):
        return (((y + k) % NY) * NH + h, t)

    def hdev(k):
        return dev((h + k) % NH, x, c)

    def tdev(k):
        return (f, (t + k) % 16)

    loads = []

    def load(src, dst):
        cp = pltpu.make_async_copy(src, dst, lsem.at[len(loads)])
        cp.start()
        loads.append(cp)
        return cp

    l_fr = load(frow_in, frow)
    l_rr = load(rrow_in, rrow)
    l_cots = load(cots_in, cots)
    l_acts = [load(acts_in.at[:, pl.ds(pl.multiple_of(j * dblk + x * 128, 128), 128)], acb.at[:, j * 128:(j + 1) * 128])
              for j in range(NY)]
    l_b = load(basis_out_in, bsrc)
    l_w = load(weight_in, weight)
    l_q = load(basis_in_in, basis_in)
    l_ein = load(eigen_in_in, ein_v)
    l_eout = load(eigen_out_in, eout_v)

    bar = pltpu.get_barrier_semaphore()
    peers = [ydev(k) for k in range(1, NY)] + [hdev(k) for k in range(1, NH)] + [tdev(k) for k in range(1, 16)]
    for p in peers:
        pl.semaphore_signal(bar, inc=1, device_id=p, device_id_type=MESH)

    count = [0]

    def sems(n):
        i = count[0]
        count[0] += n
        return i

    def rcopy(src, dst, i, to):
        return pltpu.make_async_remote_copy(
            src_ref=src, dst_ref=dst, send_sem=ssem.at[i], recv_sem=rsem.at[i],
            device_id=to, device_id_type=MESH)

    pending = []

    def push(src, dst, i, to):
        cp = rcopy(src, dst, i, to)
        cp.start()
        pending.append(cp)
        return cp

    def rows_of(slot, n):
        return pl.ds(pl.multiple_of(slot * n, 16), n)

    class Ring:
        def __init__(self, buf, stride, first, rows, part):
            self.buf, self.stride, self.first, self.rows, self.part = buf, stride, first, rows, part
            self.base = sems(8)
            self.cps = [[], []]

        def send(self, s):
            for d in range(2):
                if s:
                    self.cps[d][s - 1].wait_recv()
                slot = (y - s) % NY if d == 0 else (y + s) % NY
                lo, n = self.first, self.rows
                if s == 3:
                    lo, n = (lo, self.part) if d == 0 else (lo + self.part, n - self.part)
                sl = pl.ds(pl.multiple_of(slot * self.stride + lo, 16), n)
                self.cps[d].append(push(self.buf.at[sl], self.buf.at[sl], self.base + d * 4 + s,
                                        ydev(1 if d == 0 else NY - 1)))

        def finish(self):
            for d in range(2):
                self.cps[d][3].wait_recv()

    pool = acb.shape[0]
    l_fr.wait()
    l_rr.wait()
    ohf = (lax.broadcasted_iota(jnp.int32, (pool, fc), 0) == frow[...]).astype(BF)
    ohr = (lax.broadcasted_iota(jnp.int32, (pool, rc), 0) == rrow[...]).astype(BF)
    l_cots.wait()
    cf[rows_of(y, fc), :] = dot(ohf, cots[...], 0, 0).astype(BF)
    for cp in l_acts:
        cp.wait()
    sel = dot(ohf, acb[...], 0, 0).astype(BF)
    for j in range(NY):
        asf[j] = sel[:, j * 128:(j + 1) * 128]
    l_b.wait()
    mine_b = rows_of(h, 32)
    bz[mine_b, :] = jnp.zeros((32, cols), BF)
    bz[pl.ds(pl.multiple_of(h * 32, 16), brows), :] = bsrc[0]
    pl.semaphore_wait(bar, len(peers))

    rings_cf = [Ring(cf, fc, 0, fc // 2, fc // 4), Ring(cf, fc, fc // 2, fc // 2, fc // 4)]
    for r in rings_cf:
        r.send(0)
    i = sems(8)
    p_af = [push(asf.at[(y + k) % NY], af.at[x, rows_of(y, fc)], i + k, ydev(k)) for k in (1, 7, 2, 6, 3, 5, 4)]
    af[x, rows_of(y, fc), :] = asf[y]
    i = sems(3)
    g_b = [push(bz.at[mine_b], bz.at[mine_b], i + k - 1, hdev(k)) for k in (1, 3, 2)]
    for r in rings_cf:
        r.send(1)
    for cp in p_af:
        cp.wait_recv()
    i = sems(3)
    g_af = [push(af.at[x], af.at[x], i + k - 1, dev(h, (x + k) % NX, c)) for k in (1, 3, 2)]
    for r in rings_cf:
        r.send(2)
    cr[rows_of(y, rc), :] = dot(ohr, cots[...], 0, 0).astype(BF)
    sel = dot(ohr, acb[...], 0, 0).astype(BF)
    for j in range(NY):
        asr[j] = sel[:, j * 128:(j + 1) * 128]
    for r in rings_cf:
        r.send(3)

    for cp in g_b:
        cp.wait_recv()
    b112[...] = jnp.concatenate([bz[k * 32:k * 32 + brows, :].astype(F32) for k in range(NH)], axis=0)
    bb[rows_of(y, NH * brows), :] = b112[...].astype(BF)
    ring_b = Ring(bb, NH * brows, 0, NH * brows, 64)
    ring_b.send(0)

    for cp in g_af:
        cp.wait_recv()
    for r in rings_cf:
        r.finish()

    up, down, far = (h + 1) % NH, (h + 3) % NH, (h + 2) % NH
    for k, q in enumerate((far, up, down, h)):
        ts[q] = dot(af[q], cf[...], 0, 0).astype(BF)
        if k == 0:
            i = sems(6)
            far_up = push(ts.at[far, 0:64], tf.at[0], i, hdev(1))
            far_down = push(ts.at[far, 64:128], tf.at[1], i + 1, hdev(3))
        if k == 1:
            plain_up = push(ts.at[up, 64:128], tr.at[0, 64:128], i + 2, hdev(1))
        if k == 2:
            plain_down = push(ts.at[down, 0:64], tr.at[1, 0:64], i + 3, hdev(3))
    ring_b.send(1)
    far_up.wait_recv()
    tg[0] = (tf[0].astype(F32) + ts[up, 0:64].astype(F32)).astype(BF)
    both_up = push(tg.at[0], tr.at[0, 0:64], i + 4, hdev(1))
    far_down.wait_recv()
    tg[1] = (tf[1].astype(F32) + ts[down, 64:128].astype(F32)).astype(BF)
    both_down = push(tg.at[1], tr.at[1, 64:128], i + 5, hdev(3))

    i = sems(8)
    p_ar = [push(asr.at[(y + k) % NY], ar.at[x, rows_of(y, rc)], i + k, ydev(k)) for k in (1, 7, 2, 6, 3, 5, 4)]
    ar[x, rows_of(y, rc), :] = asr[y]
    ring_b.send(2)
    ring_b.send(3)
    ring_cr = Ring(cr, rc, 0, rc, rc // 2)
    ring_cr.send(0)
    for cp in p_ar:
        cp.wait_recv()
    i = sems(3)
    g_ar = [push(ar.at[x], ar.at[x], i + k - 1, dev(h, (x + k) % NX, c)) for k in (1, 3, 2)]

    for cp in (plain_up, plain_down, both_up, both_down):
        cp.wait_recv()
    mom = ts[h].astype(F32) + tr[0].astype(F32) + tr[1].astype(F32)
    l_q.wait()
    q_in = basis_in[0]
    rot = dot(q_in, mom.astype(BF), 0, 0).astype(BF)
    ring_cr.send(1)
    ring_b.finish()
    m2 = dot(rot, bb[...], 1, 0) / forget_count
    eye = lax.broadcasted_iota(jnp.int32, (128, 128), 0) == lax.broadcasted_iota(jnp.int32, (128, 128), 1)
    l_ein.wait()
    l_eout.wait()
    ein = jnp.sum(jnp.where(eye, ein_v[...], 0.0), axis=1, keepdims=True)
    scaled = (m2 / (ein * eout_v[...] + damping)).astype(BF)
    l_w.wait()

    parts = ((0, 512), (512, cols - 512))
    own, fwd = [], [None, None]
    ig = [sems(6), sems(6)]
    for p, (lo, n) in enumerate(parts):
        cs = pl.ds(lo, n)
        back = dot(scaled, bb[lo:lo + n, :], 1, 1).astype(BF)
        upd = dot(q_in, back, 1, 0)
        nw[h, :, lo:lo + n] = (weight[:, lo:lo + n].astype(F32) + step_size * upd).astype(BF)
        a, b = nw.at[h, 0:64, cs], nw.at[h, 64:128, cs]
        own.append([push(a, a, ig[p], hdev(1)), push(b, b, ig[p] + 1, hdev(3)),
                    push(b, b, ig[p] + 2, hdev(1)), push(a, a, ig[p] + 3, hdev(3))])

    def forward(p):
        cs = pl.ds(parts[p][0], parts[p][1])
        own[p][0].wait_recv()
        a = nw.at[down, 0:64, cs]
        one = push(a, a, ig[p] + 4, hdev(1))
        own[p][1].wait_recv()
        b = nw.at[up, 64:128, cs]
        fwd[p] = (one, push(b, b, ig[p] + 5, hdev(3)))

    igr = sems(16)

    def gradients(q):
        g = dot(cr[...], nw[q], 1, 1)
        for s in range(2):
            for p in range(2):
                ct = 2 * s + p
                gs[q * NC + ct] = jnp.concatenate(
                    [g[(4 * p + i) * rc + 16 * s:(4 * p + i) * rc + 16 * s + 16, :] for i in range(4)], axis=0).astype(BF)
                e = (q * NC + ct - t) % 16
                cp = rcopy(gs.at[q * NC + ct], gr.at[e], igr + e, dev(h, q, ct))

                @pl.when(e != 0)
                def _():
                    cp.start()

    p_r = []

    def retained(p):
        lo, n = parts[p]
        tot = dot(ar[0], nw[0, :, lo:lo + n], 1, 0)
        for q in range(1, NH):
            tot = tot + dot(ar[q], nw[q, :, lo:lo + n], 1, 0)
        for j in range(NY):
            rs[j, :, lo:lo + n] = tot[j * rc:(j + 1) * rc, :].astype(BF)
        i = sems(8)
        cs = pl.ds(lo, n)
        for k in (1, 7, 2, 6, 3, 5, 4):
            p_r.append(push(rs.at[(y + k) % NY, :, cs], rr.at[k, :, cs], i + k, ydev(k)))

    ring_cr.send(2)
    forward(0)
    ring_cr.send(3)
    for cp in g_ar:
        cp.wait_recv()
    ring_cr.finish()
    gradients(h)
    forward(1)
    for cp in (own[0][2], own[0][3]) + fwd[0]:
        cp.wait_recv()
    retained(0)
    for cp in (own[1][2], own[1][3]):
        cp.wait_recv()
    gradients(up)
    gradients(down)
    for cp in fwd[1]:
        cp.wait_recv()
    gradients(far)
    retained(1)

    gsum = gs[t].astype(F32)
    for e in range(1, 16):
        rcopy(gs.at[0], gr.at[e], igr + e, ydev(1)).wait_recv()
        gsum = gsum + gr[e].astype(F32)
    g2[...] = gsum.astype(BF)

    i2 = sems(8)
    s2 = sems(4)

    def own_part(i):
        yo = 4 * core + i
        k = (yo - y) % NY
        return k, pltpu.make_async_remote_copy(
            src_ref=g2.at[i * 16:(i + 1) * 16], dst_ref=g3.at[y], send_sem=ssem.at[s2 + i], recv_sem=rsem.at[i2 + k],
            device_id=(yo * NH + h, t), device_id_type=MESH)

    for i in range(4):
        k, cp = own_part(i)

        @pl.when(k != 0)
        def _():
            cp.start()

        @pl.when(k == 0)
        def _():
            g3[y] = g2[i * 16:(i + 1) * 16, :]

    i3 = sems(8)
    s3 = sems(16)
    mine = (y // 4) == core

    def final(k):
        return pltpu.make_async_remote_copy(
            src_ref=g3, dst_ref=go.at[2 * x + half], send_sem=ssem.at[s3 + k], recv_sem=rsem.at[i3 + 2 * x + half],
            device_id=tdev(k), device_id_type=MESH)

    @pl.when(mine)
    def _():
        for k in range(1, NY):
            rcopy(g2.at[0:16], g3.at[y], i2 + k, ydev(1)).wait_recv()
        for k in (1, 15, 2, 14, 3, 13, 4, 12, 5, 11, 6, 10, 7, 9, 8):
            final(k).start()
        go[2 * x + half] = g3[...]

    for cp in p_r:
        cp.wait_recv()
    tot = rs[y].astype(F32)
    for k in range(1, NY):
        tot = tot + rr[k].astype(F32)
    out_r[...] = tot.astype(BF)

    for cp in pending:
        cp.wait_send()
    for e in range(1, 16):
        rcopy(gs.at[0], gr.at[e], igr + e, ydev(1)).wait_send()
    for i in range(4):
        k, cp = own_part(i)

        @pl.when(k != 0)
        def _():
            cp.wait_send()

    for q in range(NX):
        for s in range(2):
            @pl.when(jnp.logical_not(jnp.logical_and(mine, 2 * x + half == 2 * q + s)))
            def _():
                rcopy(g3, go.at[2 * q + s], i3 + 2 * q + s, ydev(1)).wait_recv()
            for j in range(NY):
                lo = j * dblk + q * 128
                out_g[16 * s:16 * s + 16, lo:lo + 128] = go[2 * q + s, j]

    @pl.when(mine)
    def _():
        for k in range(1, 16):
            final(k).wait_send()
    assert count[0] <= NSEM


def shards(acts, cots, weight, basis_in, basis_out, eigen_in, eigen_out, forget_rows, retain_rows):
    fc, rc = forget_rows.shape[0], retain_rows.shape[0]
    pool, cols = cots.shape
    dim = acts.shape[1]
    dblk = dim // NY
    brows = basis_out.shape[1]
    vm = lambda *s: pltpu.VMEM(s, BF)
    vf = lambda *s: pltpu.VMEM(s, F32)
    kern = functools.partial(body, fc, rc, cols, dblk, brows, float(fc * NY * NH))
    return pl.pallas_call(
        kern,
        out_shape=(jax.ShapeDtypeStruct((rc, cols), BF), jax.ShapeDtypeStruct((rc, dim), BF)),
        in_specs=[pl.BlockSpec(memory_space=pl.ANY)] * 9,
        out_specs=(pl.BlockSpec(memory_space=pltpu.VMEM),) * 2,
        scratch_shapes=[
            vm(pool, NY * 128), vm(pool, cols), vm(128, cols), vm(1, 128, 128), vm(1, brows, cols),
            vf(1, 128), vf(1, cols), pltpu.VMEM((1, fc), jnp.int32), pltpu.VMEM((1, rc), jnp.int32),
            vm(NH, NY * fc, 128), vm(NH, NY * rc, 128), vm(NY, fc, 128), vm(NY, rc, 128),
            vm(NY * fc, cols), vm(NY * rc, cols),
            vm(NH * 32, cols), vf(NH * brows, cols), vm(cols, cols),
            vm(NH, 128, cols), vm(2, 64, cols), vm(2, 64, cols), vm(2, 128, cols), vm(NH, 128, cols),
            vm(NY, rc, cols), vm(NY, rc, cols),
            vm(16, 64, 128), vm(16, 64, 128), vm(64, 128), vm(NY, 16, 128), vm(2 * NX, NY, 16, 128),
            pltpu.SemaphoreType.DMA((20,)), pltpu.SemaphoreType.DMA((NSEM,)), pltpu.SemaphoreType.DMA((NSEM,)),
        ],
        compiler_params=pltpu.CompilerParams(collective_id=0, has_side_effects=True, vmem_limit_bytes=62 * 2**20),
        name="newton_step",
    )(acts, cots, weight, basis_in, basis_out, eigen_in.reshape(1, -1), eigen_out.reshape(1, -1),
      forget_rows.reshape(1, -1), retain_rows.reshape(1, -1))


def solution(mesh):
    placed = (
        P("fsdp", None),
        P("fsdp", "tp"),
        P("fsdp", "tp"),
        P("fsdp", None, None),
        P("tp", "fsdp", None),
        P("fsdp"),
        P("tp"),
        P("fsdp"),
        P("fsdp"),
    )
    return jax.shard_map(
        shards,
        mesh=mesh,
        in_specs=placed,
        out_specs=(P("fsdp", "tp"), P("fsdp", None)),
        check_vma=False,
    )
```

time: 667 us -> 97.1 us (0.15)
  waiting for transfers between devices: 587 us -> 0 us
  Pallas kernels: 0 us -> 91.9 us
  blocking collectives: 23 us -> 0 us
  starting transfers between devices: 14.7 us -> 0 us
  matrix products: 13.5 us -> 0 us
  between operations: 13.9 us -> 0.64 us
    all_gather x3 -> x0, waiting for transfers between devices: 243 us -> none  [the longest x1 98.4 us: shards(): basis_full = lax.all_gather(basis_out, 'fsdp', axis=1, tiled=True)]
    reduce_scatter x1 -> x0, waiting for transfers between devices: 205 us -> none  [shards(): lax.psum_scatter(jnp.dot(retain_cols, new_weight, preferred_element_type=...]
    psum x1 -> x0, waiting for transfers between devices: 124 us -> none  [shards(): grad_summed = lax.psum(grad_cols.astype(jnp.bfloat16), 'tp')]
    pallas_call x0 -> x1, Pallas kernels: none -> 91.9 us  [shards(): pl.pallas_call(kern, out_shape=(jax.ShapeDtypeStruct((rc, cols), BF), jax...]
    all_to_all x1 -> x0, blocking collectives: 23 us -> none  [shards(): lax.all_to_all(grad_summed, 'fsdp', split_axis=0, concat_axis=1, tiled=True)]
    all_to_all x2 -> x0, waiting for transfers between devices: 14.6 us -> none  [the longest x1 14.6 us: shards(): lax.all_to_all(forget_acts, 'fsdp', split_axis=1, concat_axis=0, tiled=True)]
    all_to_all x2 -> x0, starting transfers between devices: 14.5 us -> none  [the longest x1 8.03 us: shards(): lax.all_to_all(retain_acts, 'fsdp', split_axis=1, concat_axis=0, tiled=True)]
    dot_general x5 -> x0, matrix products: 13.5 us -> none  [the longest x1 3.04 us: shards(): lax.dot_general(rotated_acts, lax.all_gather(rotated_cots, 'fsdp', axis=0...]
  transfers between devices with their start and end apart: 7 -> 0, of which waited for: 6 -> 0; matrix products, arithmetic and copies ran while one was open for 3% -> 0% of each run, Pallas kernels for 0% -> 0%
where the time goes in v2:
time: 97.1 us; the launch traced here: 96.9 us
  Pallas kernels  91.9 us (95%)
  local copies, waits for them, and re-layouts  4.38 us (5%)
    pallas_call x1, Pallas kernels, shards(): pl.pallas_call(kern, out_shape=(jax.ShapeDtypeStruct((rc, cols), BF), jax...  91.9 us
    unnamed x2, local copies, waits for them, and re-layouts  3.12 us

profile of v2, /device:TPU:1, one launch (start us, length us, event | category | flops | bytes accessed | tf_op | source)
XLA Modules:
  0.0 96.9 jit_solution(14795806911373745311)
XLA Ops:
  0.6 1.3 %reshape.17.eigen_out_in = f32[1,896]{1,0:T(1,128)} reshape(f32[896]{0:T(1024)} %param.15) | data formatting | bytes 7168 | tf_op jit(solution)/shard_map/reshape | solution.py:392
  1.9 91.9 %newton_step.1 = (bf16[32,896]{1,0:T(8,128)(2,1)}, bf16[32,4096]{1,0:T(8,128)(2,1)}) custom-call(bf16[256,4096]{1,0:T(8,128)(2,1)} %acts_in.1, bf16[256,896]{1,0:T(8,128)(2,1)} %cots_in.1, bf16[128,896]{1,0:T(8,128)(2,1)} %weight_in.1, bf16[1,128,128]{2,1,0:T(8,128)(2,1)} %basis_in_in.1, bf16[1,28,896]{2,1,0:T(8,128)(2,1)} %basis_out_in.1, ...), custom_call_target="tpu_custom_call" | custom-call | tf_op jit(solution)/shard_map/newton_step/pallas_call | solution.py:374
  93.8 1.4 %copy.13 = bf16[32,896]{1,0:T(8,128)(2,1)} copy(bf16[32,896]{1,0:T(8,128)(2,1)} %get-tuple-element.4) | data formatting | bytes 114688
  95.2 1.7 %copy.14 = bf16[32,4096]{1,0:T(8,128)(2,1)} copy(bf16[32,4096]{1,0:T(8,128)(2,1)} %get-tuple-element.5) | data formatting | bytes 524288

commit v3 on v2

--- a/solution.py
+++ b/solution.py
@@ -92,8 +92,10 @@
         return pl.ds(pl.multiple_of(slot * n, 16), n)
 
     class Ring:
-        def __init__(self, buf, stride, first, rows, part):
-            self.buf, self.stride, self.first, self.rows, self.part = buf, stride, first, rows, part
+        def __init__(self, buf, rows, part, first=0, n=None, cs=None):
+            self.buf, self.rows, self.part = buf, rows, part
+            self.first, self.n = first, rows if n is None else n
+            self.cs = pl.ds(0, cols) if cs is None else cs
             self.base = sems(8)
             self.cps = [[], []]
 
@@ -102,12 +104,11 @@
                 if s:
                     self.cps[d][s - 1].wait_recv()
                 slot = (y - s) % NY if d == 0 else (y + s) % NY
-                lo, n = self.first, self.rows
+                lo, n = self.first, self.n
                 if s == 3:
                     lo, n = (lo, self.part) if d == 0 else (lo + self.part, n - self.part)
-                sl = pl.ds(pl.multiple_of(slot * self.stride + lo, 16), n)
-                self.cps[d].append(push(self.buf.at[sl], self.buf.at[sl], self.base + d * 4 + s,
-                                        ydev(1 if d == 0 else NY - 1)))
+                sl = self.buf.at[pl.ds(pl.multiple_of(slot * self.rows + lo, 16), n), self.cs]
+                self.cps[d].append(push(sl, sl, self.base + d * 4 + s, ydev(1 if d == 0 else NY - 1)))
 
         def finish(self):
             for d in range(2):
@@ -131,89 +132,99 @@
     bz[pl.ds(pl.multiple_of(h * 32, 16), brows), :] = bsrc[0]
     pl.semaphore_wait(bar, len(peers))
 
-    rings_cf = [Ring(cf, fc, 0, fc // 2, fc // 4), Ring(cf, fc, fc // 2, fc // 2, fc // 4)]
+    parts = ((0, 512), (512, cols - 512))
+    i = sems(8)
+    p_af = [push(asf.at[(y + k) % NY], af.at[x, rows_of(y, fc)], i + k, ydev(k)) for k in (1, 7, 2, 6, 3, 5, 4)]
+    rings_cf = [Ring(cf, fc, fc // 2, cs=pl.ds(lo, n)) for lo, n in parts]
     for r in rings_cf:
         r.send(0)
-    i = sems(8)
-    p_af = [push(asf.at[(y + k) % NY], af.at[x, rows_of(y, fc)], i + k, ydev(k)) for k in (1, 7, 2, 6, 3, 5, 4)]
-    af[x, rows_of(y, fc), :] = asf[y]
     i = sems(3)
     g_b = [push(bz.at[mine_b], bz.at[mine_b], i + k - 1, hdev(k)) for k in (1, 3, 2)]
-    for r in rings_cf:
-        r.send(1)
+    af[x, rows_of(y, fc), :] = asf[y]
+    sel = dot(ohr, acb[...], 0, 0).astype(BF)
+    for j in range(NY):
+        asr[j] = sel[:, j * 128:(j + 1) * 128]
+    cr[rows_of(y, rc), :] = dot(ohr, cots[...], 0, 0).astype(BF)
     for cp in p_af:
         cp.wait_recv()
     i = sems(3)
     g_af = [push(af.at[x], af.at[x], i + k - 1, dev(h, (x + k) % NX, c)) for k in (1, 3, 2)]
     for r in rings_cf:
+        r.send(1)
+    i = sems(8)
+    p_ar = [push(asr.at[(y + k) % NY], ar.at[x, rows_of(y, rc)], i + k, ydev(k)) for k in (1, 7, 2, 6, 3, 5, 4)]
+    ring_cr = Ring(cr, rc, rc // 2)
+    ring_cr.send(0)
+    ar[x, rows_of(y, rc), :] = asr[y]
+    for cp in g_b:
+        cp.wait_recv()
+    b112[...] = jnp.concatenate([bz[k * 32:k * 32 + brows, :].astype(F32) for k in range(NH)], axis=0)
+    bb[rows_of(y, NH * brows), :] = b112[...].astype(BF)
+    rings_b = [Ring(bb, NH * brows, 32, 0, 64), Ring(bb, NH * brows, 32, 64, NH * brows - 64)]
+    for r in rings_cf:
         r.send(2)
-    cr[rows_of(y, rc), :] = dot(ohr, cots[...], 0, 0).astype(BF)
-    sel = dot(ohr, acb[...], 0, 0).astype(BF)
-    for j in range(NY):
-        asr[j] = sel[:, j * 128:(j + 1) * 128]
+    ring_cr.send(1)
     for r in rings_cf:
         r.send(3)
-
-    for cp in g_b:
-        cp.wait_recv()
-    b112[...] = jnp.concatenate([bz[k * 32:k * 32 + brows, :].astype(F32) for k in range(NH)], axis=0)
-    bb[rows_of(y, NH * brows), :] = b112[...].astype(BF)
-    ring_b = Ring(bb, NH * brows, 0, NH * brows, 64)
-    ring_b.send(0)
-
+    for r in rings_b:
+        r.send(0)
+    for cp in p_ar:
+        cp.wait_recv()
+    i = sems(3)
     for cp in g_af:
         cp.wait_recv()
-    for r in rings_cf:
-        r.finish()
+    g_ar = [push(ar.at[x], ar.at[x], i + k - 1, dev(h, (x + k) % NX, c)) for k in (1, 3, 2)]
 
     up, down, far = (h + 1) % NH, (h + 3) % NH, (h + 2) % NH
-    for k, q in enumerate((far, up, down, h)):
-        ts[q] = dot(af[q], cf[...], 0, 0).astype(BF)
-        if k == 0:
-            i = sems(6)
-            far_up = push(ts.at[far, 0:64], tf.at[0], i, hdev(1))
-            far_down = push(ts.at[far, 64:128], tf.at[1], i + 1, hdev(3))
-        if k == 1:
-            plain_up = push(ts.at[up, 64:128], tr.at[0, 64:128], i + 2, hdev(1))
-        if k == 2:
-            plain_down = push(ts.at[down, 0:64], tr.at[1, 0:64], i + 3, hdev(3))
-    ring_b.send(1)
-    far_up.wait_recv()
-    tg[0] = (tf[0].astype(F32) + ts[up, 0:64].astype(F32)).astype(BF)
-    both_up = push(tg.at[0], tr.at[0, 0:64], i + 4, hdev(1))
-    far_down.wait_recv()
-    tg[1] = (tf[1].astype(F32) + ts[down, 64:128].astype(F32)).astype(BF)
-    both_down = push(tg.at[1], tr.at[1, 64:128], i + 5, hdev(3))
-
-    i = sems(8)
-    p_ar = [push(asr.at[(y + k) % NY], ar.at[x, rows_of(y, rc)], i + k, ydev(k)) for k in (1, 7, 2, 6, 3, 5, 4)]
-    ar[x, rows_of(y, rc), :] = asr[y]
-    ring_b.send(2)
-    ring_b.send(3)
-    ring_cr = Ring(cr, rc, 0, rc, rc // 2)
-    ring_cr.send(0)
-    for cp in p_ar:
-        cp.wait_recv()
-    i = sems(3)
-    g_ar = [push(ar.at[x], ar.at[x], i + k - 1, dev(h, (x + k) % NX, c)) for k in (1, 3, 2)]
-
-    for cp in (plain_up, plain_down, both_up, both_down):
+    its, first = [], []
+    for p, (lo, n) in enumerate(parts):
+        cs = pl.ds(lo, n)
+        rings_cf[p].finish()
+        i = sems(6)
+        its.append(i)
+        ts[far, :, lo:lo + n] = dot(af[far], cf[:, lo:lo + n], 0, 0).astype(BF)
+        far_up = push(ts.at[far, 0:64, cs], tf.at[0, :, cs], i, hdev(1))
+        far_down = push(ts.at[far, 64:128, cs], tf.at[1, :, cs], i + 1, hdev(3))
+        ts[up, :, lo:lo + n] = dot(af[up], cf[:, lo:lo + n], 0, 0).astype(BF)
+        plain_up = push(ts.at[up, 64:128, cs], tr.at[0, 64:128, cs], i + 2, hdev(1))
+        ts[down, :, lo:lo + n] = dot(af[down], cf[:, lo:lo + n], 0, 0).astype(BF)
+        plain_down = push(ts.at[down, 0:64, cs], tr.at[1, 0:64, cs], i + 3, hdev(3))
+        first.append((far_up, far_down, plain_up, plain_down))
+        ts[h, :, lo:lo + n] = dot(af[h], cf[:, lo:lo + n], 0, 0).astype(BF)
+    for r in rings_b:
+        r.send(1)
+    ring_cr.send(2)
+    last = []
+    for p, (lo, n) in enumerate(parts):
+        cs = pl.ds(lo, n)
+        first[p][0].wait_recv()
+        tg[0, :, lo:lo + n] = (tf[0, :, lo:lo + n].astype(F32) + ts[up, 0:64, lo:lo + n].astype(F32)).astype(BF)
+        last.append(push(tg.at[0, :, cs], tr.at[0, 0:64, cs], its[p] + 4, hdev(1)))
+        first[p][1].wait_recv()
+        tg[1, :, lo:lo + n] = (tf[1, :, lo:lo + n].astype(F32) + ts[down, 64:128, lo:lo + n].astype(F32)).astype(BF)
+        last.append(push(tg.at[1, :, cs], tr.at[1, 64:128, cs], its[p] + 5, hdev(3)))
+        for r in rings_b:
+            r.send(2 + p)
+    ring_cr.send(3)
+    for p in range(2):
+        first[p][2].wait_recv()
+        first[p][3].wait_recv()
+    for cp in last:
         cp.wait_recv()
     mom = ts[h].astype(F32) + tr[0].astype(F32) + tr[1].astype(F32)
     l_q.wait()
     q_in = basis_in[0]
     rot = dot(q_in, mom.astype(BF), 0, 0).astype(BF)
-    ring_cr.send(1)
-    ring_b.finish()
+    for r in rings_b:
+        r.finish()
     m2 = dot(rot, bb[...], 1, 0) / forget_count
     eye = lax.broadcasted_iota(jnp.int32, (128, 128), 0) == lax.broadcasted_iota(jnp.int32, (128, 128), 1)
     l_ein.wait()
     l_eout.wait()
     ein = jnp.sum(jnp.where(eye, ein_v[...], 0.0), axis=1, keepdims=True)
-    scaled = (m2 / (ein * eout_v[...] + damping)).astype(BF)
+    scaled = (m2 / (ein * eout_v[...].reshape(1, cols) + damping)).astype(BF)
     l_w.wait()
 
-    parts = ((0, 512), (512, cols - 512))
     own, fwd = [], [None, None]
     ig = [sems(6), sems(6)]
     for p, (lo, n) in enumerate(parts):
@@ -264,9 +275,7 @@
         for k in (1, 7, 2, 6, 3, 5, 4):
             p_r.append(push(rs.at[(y + k) % NY, :, cs], rr.at[k, :, cs], i + k, ydev(k)))
 
-    ring_cr.send(2)
     forward(0)
-    ring_cr.send(3)
     for cp in g_ar:
         cp.wait_recv()
     ring_cr.finish()
@@ -378,7 +387,7 @@
         out_specs=(pl.BlockSpec(memory_space=pltpu.VMEM),) * 2,
         scratch_shapes=[
             vm(pool, NY * 128), vm(pool, cols), vm(128, cols), vm(1, 128, 128), vm(1, brows, cols),
-            vf(1, 128), vf(1, cols), pltpu.VMEM((1, fc), jnp.int32), pltpu.VMEM((1, rc), jnp.int32),
+            vf(1, 128), vf(cols), pltpu.VMEM((1, fc), jnp.int32), pltpu.VMEM((1, rc), jnp.int32),
             vm(NH, NY * fc, 128), vm(NH, NY * rc, 128), vm(NY, fc, 128), vm(NY, rc, 128),
             vm(NY * fc, cols), vm(NY * rc, cols),
             vm(NH * 32, cols), vf(NH * brows, cols), vm(cols, cols),
@@ -389,7 +398,7 @@
         ],
         compiler_params=pltpu.CompilerParams(collective_id=0, has_side_effects=True, vmem_limit_bytes=62 * 2**20),
         name="newton_step",
-    )(acts, cots, weight, basis_in, basis_out, eigen_in.reshape(1, -1), eigen_out.reshape(1, -1),
+    )(acts, cots, weight, basis_in, basis_out, eigen_in.reshape(1, -1), eigen_out,
       forget_rows.reshape(1, -1), retain_rows.reshape(1, -1))
 
 

time: 97.1 us -> 94.6 us (0.974)
  Pallas kernels: 91.9 us -> 90.6 us
  local copies, waits for them, and re-layouts: 4.38 us -> 3.12 us
    reshape x1 -> x0, local copies, waits for them, and re-layouts: 1.27 us -> none  [shards(): eigen_out.reshape(1, -1)]
    pallas_call x1, Pallas kernels: 91.9 us -> 90.6 us  [shards(): pl.pallas_call(kern, out_shape=(jax.ShapeDtypeStruct((rc, cols), BF), jax...]
where the time goes in v3:
time: 94.6 us; the launch traced here: 94.4 us
  Pallas kernels  90.6 us (96%)
  local copies, waits for them, and re-layouts  3.12 us (3%)
    pallas_call x1, Pallas kernels, shards(): pl.pallas_call(kern, out_shape=(jax.ShapeDtypeStruct((rc, cols), BF), jax...  90.6 us
    unnamed x2, local copies, waits for them, and re-layouts  3.12 us

profile of v3, /device:TPU:1, one launch (start us, length us, event | category | flops | bytes accessed | tf_op | source)
XLA Modules:
  0.0 94.4 jit_solution(15669682678101915745)
XLA Ops:
  0.6 90.6 %newton_step.1 = (bf16[32,896]{1,0:T(8,128)(2,1)}, bf16[32,4096]{1,0:T(8,128)(2,1)}) custom-call(bf16[256,4096]{1,0:T(8,128)(2,1)} %acts_in.1, bf16[256,896]{1,0:T(8,128)(2,1)} %cots_in.1, bf16[128,896]{1,0:T(8,128)(2,1)} %weight_in.1, bf16[1,128,128]{2,1,0:T(8,128)(2,1)} %basis_in_in.1, bf16[1,28,896]{2,1,0:T(8,128)(2,1)} %basis_out_in.1, ...), custom_call_target="tpu_custom_call" | custom-call | tf_op jit(solution)/shard_map/newton_step/pallas_call | solution.py:383
  91.2 1.4 %copy.13 = bf16[32,896]{1,0:T(8,128)(2,1)} copy(bf16[32,896]{1,0:T(8,128)(2,1)} %get-tuple-element.4) | data formatting | bytes 114688
  92.7 1.7 %copy.14 = bf16[32,4096]{1,0:T(8,128)(2,1)} copy(bf16[32,4096]{1,0:T(8,128)(2,1)} %get-tuple-element.5) | data formatting | bytes 524288

commit v4 on v3

--- a/solution.py
+++ b/solution.py
@@ -191,9 +191,9 @@
         plain_down = push(ts.at[down, 0:64, cs], tr.at[1, 0:64, cs], i + 3, hdev(3))
         first.append((far_up, far_down, plain_up, plain_down))
         ts[h, :, lo:lo + n] = dot(af[h], cf[:, lo:lo + n], 0, 0).astype(BF)
+    ring_cr.send(2)
     for r in rings_b:
         r.send(1)
-    ring_cr.send(2)
     last = []
     for p, (lo, n) in enumerate(parts):
         cs = pl.ds(lo, n)
@@ -291,7 +291,6 @@
     for cp in fwd[1]:
         cp.wait_recv()
     gradients(far)
-    retained(1)
 
     gsum = gs[t].astype(F32)
     for e in range(1, 16):
@@ -319,6 +318,8 @@
         @pl.when(k == 0)
         def _():
             g3[y] = g2[i * 16:(i + 1) * 16, :]
+
+    retained(1)
 
     i3 = sems(8)
     s3 = sems(16)

time: 94.6 us -> 94.5 us (level)
  no operation moved by 1% of the time
where the time goes in v4:
time: 94.5 us; the launch traced here: 94.3 us
  Pallas kernels  90.5 us (96%)
  local copies, waits for them, and re-layouts  3.12 us (3%)
    pallas_call x1, Pallas kernels, shards(): pl.pallas_call(kern, out_shape=(jax.ShapeDtypeStruct((rc, cols), BF), jax...  90.5 us
    unnamed x2, local copies, waits for them, and re-layouts  3.12 us

profile of v4, /device:TPU:1, one launch (start us, length us, event | category | flops | bytes accessed | tf_op | source)
XLA Modules:
  0.0 94.3 jit_solution(10944204121081600195)
XLA Ops:
  0.6 90.5 %newton_step.1 = (bf16[32,896]{1,0:T(8,128)(2,1)}, bf16[32,4096]{1,0:T(8,128)(2,1)}) custom-call(bf16[256,4096]{1,0:T(8,128)(2,1)} %acts_in.1, bf16[256,896]{1,0:T(8,128)(2,1)} %cots_in.1, bf16[128,896]{1,0:T(8,128)(2,1)} %weight_in.1, bf16[1,128,128]{2,1,0:T(8,128)(2,1)} %basis_in_in.1, bf16[1,28,896]{2,1,0:T(8,128)(2,1)} %basis_out_in.1, ...), custom_call_target="tpu_custom_call" | custom-call | tf_op jit(solution)/shard_map/newton_step/pallas_call | solution.py:384
  91.2 1.4 %copy.13 = bf16[32,896]{1,0:T(8,128)(2,1)} copy(bf16[32,896]{1,0:T(8,128)(2,1)} %get-tuple-element.4) | data formatting | bytes 114688
  92.6 1.7 %copy.14 = bf16[32,4096]{1,0:T(8,128)(2,1)} copy(bf16[32,4096]{1,0:T(8,128)(2,1)} %get-tuple-element.5) | data formatting | bytes 524288
